TPU v7x, 32 devices: a whole 2x2x4 slice. The times are simulated.
32 devices in a mesh: grp: 2 (over y), blk: 4 (over z), head: 4 (over x, core).
Axes of the slice: x: 2, y: 2, z: 4, core: 2. Of those that a mesh axis runs over, the one named last changes fastest.
Arguments:
- queries: bfloat16 [8, 576, 4096], P('grp', None, ('head', 'blk')), parts along dimension 0, may hold values from -8 to 8
- tree_keys: bfloat16 [8, 32, 576], P('grp'), parts along dimension 0, may hold values from -8 to 8
- parents: int32 [8, 32], P('grp'), parts along dimension 0, may hold values from 0 to 30, as said below
- node_live: int32 [8, 32], P('grp'), parts along dimension 0, may hold values 0 or 1
- lengths: int32 [8], P('grp'), parts along dimension 0, may hold values from 1 to 6144, 15360 in all
- start_device: int32 [8], P('grp'), parts along dimension 0, may hold values from 0 to 3
- cache_latent: bfloat16 [8, 6144, 512], P('grp', 'blk'), parts along dimension 0, may hold values from -8 to 8
- cache_rope: bfloat16 [8, 64, 6144], P('grp', None, 'blk'), parts along dimension 0, may hold values from -8 to 8
- up_weight: bfloat16 [128, 512, 128], P('head'), may hold values from -1 to 1
Outputs:
- verified: bfloat16 [8, 32, 16384], P('grp', None, ('head', 'blk')), parts along dimension 0
There are 2 independent parts, one for each index of `grp`. A program takes and returns all parts, laid end to end along the dimension named above; an argument that names none is the same for every part. Nothing has to cross between parts.
Inputs may be any that keep to these rules, and one draw needn't show every extreme that they name: Together the lengths fill 5/8 of the cycle's slots; one request has exactly 6144 tokens. parents[r, 0] = 0; every other node's parent has a lower index.
All inputs are finite; a program needn't handle non-finite values.
Results may differ from a plain program's by a relative error of at most 0.012.
Values may be sent and summed in bfloat16 or wider, within the bound.
A program may use at most 128 MiB of HBM per device.

v0:
```python
import functools
import math

import jax
import jax.numpy as jnp
from jax import lax
from jax.experimental import pallas as pl
from jax.experimental.pallas import tpu as pltpu
from jax.sharding import PartitionSpec as P

DN = 128
NEGATIVE = -1e30
FLOOR = -1e29
LANES = 128


def kernel(
    n,
    peers,
    moved,
    scale,
    q_hbm,
    tree_ref,
    parent_ref,
    alive_ref,
    length_ref,
    first_ref,
    lat_hbm,
    rope_hbm,
    w_hbm,
    out_ref,
    qbuf,
    lat,
    rope,
    w,
    parts,
    mine,
    reach,
    top_ref,
    sum_ref,
    acc_ref,
    load_sem,
    w_sem,
    q_send,
    q_recv,
    p_send,
    p_recv,
    page_send,
    peer_send,
    page_recv,
):
    me = lax.axis_index("blk")
    lane_me = lax.axis_index("head")
    requests, _, cols = q_hbm.shape
    nodes = tree_ref.shape[1]
    dim_lat = lat.shape[2]
    page = lat.shape[1]
    dim_v = w.shape[2]
    heads = cols // nodes
    width = heads * dim_v
    kept = requests - moved
    share = page // peers
    mesh_id = pl.DeviceIdType.MESH
    at_end = jnp.logical_or(me == 0, me == n - 1)
    near_end = jnp.logical_or(me == 1, me == n - 2)
    end_side = jnp.where(me <= 1, 0, n - 1)

    def load_copies(r):
        return (
            pltpu.make_async_copy(q_hbm.at[r], qbuf.at[me, r], load_sem.at[0, r]),
            pltpu.make_async_copy(lat_hbm.at[r], lat.at[r], load_sem.at[1, r]),
            pltpu.make_async_copy(rope_hbm.at[r], rope.at[r], load_sem.at[2, r]),
        )

    def w_copy():
        return pltpu.make_async_copy(w_hbm, w, w_sem)

    def own_copy(r, side):
        return pltpu.make_async_remote_copy(
            src_ref=q_hbm.at[r],
            dst_ref=qbuf.at[me, r],
            send_sem=q_send.at[side, me, r],
            recv_sem=q_recv.at[me, r],
            device_id={"blk": me + 1 - 2 * side},
            device_id_type=mesh_id,
        )

    def hop_copy(origin, r, side):
        return pltpu.make_async_remote_copy(
            src_ref=qbuf.at[origin, r],
            dst_ref=qbuf.at[origin, r],
            send_sem=q_send.at[side, origin, r],
            recv_sem=q_recv.at[origin, r],
            device_id={"blk": me + 1 - 2 * side},
            device_id_type=mesh_id,
        )

    def part_copy(origin, r, holder):
        return pltpu.make_async_remote_copy(
            src_ref=mine.at[origin, r],
            dst_ref=parts.at[holder, r],
            send_sem=p_send.at[origin, r],
            recv_sem=p_recv.at[holder, r],
            device_id={"blk": origin},
            device_id_type=mesh_id,
        )

    def rows_of(j):
        return pl.ds(pl.multiple_of(j * share, share), share)

    def page_copies(g):
        inner = jnp.where(me == 0, 1, n - 2)
        mine_rows = rows_of(lane_me)
        return (
            pltpu.make_async_remote_copy(
                src_ref=lat_hbm.at[kept + g, mine_rows],
                dst_ref=lat.at[requests + g, mine_rows],
                send_sem=page_send.at[0, g],
                recv_sem=page_recv.at[0, g, lane_me],
                device_id={"blk": inner},
                device_id_type=mesh_id,
            ),
            pltpu.make_async_remote_copy(
                src_ref=rope_hbm.at[kept + g, :, mine_rows],
                dst_ref=rope.at[requests + g, :, mine_rows],
                send_sem=page_send.at[1, g],
                recv_sem=page_recv.at[1, g, lane_me],
                device_id={"blk": inner},
                device_id_type=mesh_id,
            ),
        )

    def peer_copies(g, j, peer):
        share_rows = rows_of(j)
        return tuple(
            pltpu.make_async_remote_copy(
                src_ref=view,
                dst_ref=view,
                send_sem=peer_send.at[i, g, peer],
                recv_sem=page_recv.at[i, g, j],
                device_id={"head": peer},
                device_id_type=mesh_id,
            )
            for i, view in enumerate(
                (lat.at[requests + g, share_rows], rope.at[requests + g, :, share_rows])
            )
        )

    barrier = pltpu.get_barrier_semaphore()

    @pl.loop(1, n)
    def _(k):
        pl.semaphore_signal(
            barrier, inc=1, device_id={"blk": lax.rem(me + k, n)}, device_id_type=mesh_id
        )

    if moved:

        @pl.loop(1, peers)
        def _(k):
            pl.semaphore_signal(
                barrier,
                inc=1,
                device_id={"head": lax.rem(lane_me + k, peers)},
                device_id_type=mesh_id,
            )

    @pl.loop(0, requests)
    def _(r):
        for copy in load_copies(r):
            copy.start()

    w_copy().start()
    pl.semaphore_wait(barrier, n - 1 + (peers - 1 if moved else 0))

    def sends_on(r, side):
        ahead = me + 1 - 2 * side
        valid = jnp.logical_and(ahead >= 0, ahead < n)
        if moved:
            last = jnp.logical_or(ahead == 0, ahead == n - 1)
            valid = jnp.logical_and(valid, jnp.logical_not(jnp.logical_and(last, r >= kept)))
        return valid

    if moved:

        @pl.when(at_end)
        def _():
            @pl.loop(0, moved)
            def _(g):
                for copy in page_copies(g):
                    copy.start()

    @pl.loop(0, requests)
    def _(r):
        for side in (0, 1):

            @pl.when(sends_on(r, side))
            def _():
                own_copy(r, side).start()

    lane = lax.broadcasted_iota(jnp.int32, (nodes, LANES), 1)
    total = requests * nodes
    column = lax.broadcasted_iota(jnp.int32, (total, total), 1)
    row = lax.broadcasted_iota(jnp.int32, (total, total), 0)
    parent = jnp.concatenate(
        [parent_ref[r : r + 1, :] + r * nodes for r in range(requests)], axis=1
    )
    reached = jnp.where(jnp.logical_or(parent == row, row == column), 1.0, 0.0)
    for _ in range(max(nodes - 1, 1).bit_length()):
        factor = reached.astype(jnp.bfloat16)
        reached = jnp.minimum(jnp.dot(factor, factor, preferred_element_type=jnp.float32), 1.0)
    reach[...] = reached.T.reshape(requests, nodes, total)

    if moved:
        for end in (0, n - 1):

            @pl.when(me != end)
            def _():
                @pl.loop(0, moved)
                def _(g):
                    blank = parts.at[end, kept + g]
                    blank[:, :width] = jnp.zeros((nodes, width), jnp.bfloat16)
                    blank[:, width:] = jnp.where(lane < heads, NEGATIVE, 0.0).astype(jnp.bfloat16)

    def stats(scores, values):
        top = jnp.maximum(jnp.max(scores, axis=1, keepdims=True), FLOOR)
        weights = jnp.exp2(scores - top)
        summed = jnp.sum(weights, axis=1, keepdims=True)
        acc = jnp.dot(weights.astype(jnp.bfloat16), values, preferred_element_type=jnp.float32)
        return top, summed, acc

    def page_scores(q, place, r, holder):
        s = lax.dot_general(
            q[:, :dim_lat], lat[place], (((1,), (1,)), ((), ())), preferred_element_type=jnp.float32
        )
        s = s + jnp.dot(q[:, dim_lat:], rope[place], preferred_element_type=jnp.float32)
        turn = lax.rem(holder - first_ref[r] + n, n)
        live = length_ref[r] - turn * page
        slot = lax.broadcasted_iota(jnp.int32, (1, page), 1)
        return jnp.where(slot < live, s * scale, NEGATIVE)

    def finish(top, summed, acc, origin, dst):
        any_kept = summed > 0.0
        safe = jnp.where(any_kept, summed, 1.0)
        rows = (acc * jnp.where(any_kept, 1.0 / safe, 0.0)).astype(jnp.bfloat16)
        lse = jnp.where(any_kept, top + jnp.log2(safe), NEGATIVE)
        stat = jnp.zeros((nodes, LANES), jnp.float32)
        for h in range(heads):
            span = slice(h * nodes, (h + 1) * nodes)
            projected = jnp.dot(
                rows[span], w[origin * heads + h], preferred_element_type=jnp.float32
            )
            dst[:, h * dim_v : (h + 1) * dim_v] = projected.astype(jnp.bfloat16)
            stat = jnp.where(lane % heads == h, lse[span], stat)
        high = stat.astype(jnp.bfloat16)
        rest = stat - high.astype(jnp.float32)
        middle = rest.astype(jnp.bfloat16)
        low = (rest - middle.astype(jnp.float32)).astype(jnp.bfloat16)
        packed = jnp.where(
            lane < heads,
            high.astype(jnp.float32),
            jnp.where(lane < 2 * heads, middle.astype(jnp.float32), low.astype(jnp.float32)),
        )
        dst[:, width : width + LANES] = packed.astype(jnp.bfloat16)

    w_copy().wait()

    @pl.loop(0, requests)
    def _(r):
        for copy in load_copies(r):
            copy.wait()
        q = qbuf[me, r].T
        keys = tree_ref[...].reshape(total, tree_ref.shape[2])
        s = lax.dot_general(q, keys, (((1,), (1,)), ((), ())), preferred_element_type=jnp.float32)
        seen = jnp.concatenate([reach[r]] * heads, axis=0) > 0.5
        s = jnp.where(seen, s * scale, NEGATIVE)
        top, summed, acc = stats(s, keys[:, :dim_lat])
        finish(top, summed, acc, me, parts.at[me, r])

    near = 2 * requests
    steps = near * (n - 1) + requests

    def place(u):
        v = u - kept
        late = v >= near
        own = jnp.logical_or(v < 0, jnp.logical_and(late, v < near + moved))
        t = jnp.where(late, v - moved, jnp.maximum(v, 0))
        d = t // near + 1
        side = lax.rem(t, 2)
        r = jnp.where(
            own, jnp.where(late, kept + v - near, u), lax.rem(t // 2, requests)
        )
        origin = jnp.where(own, me, me - d + 2 * d * side)
        valid = jnp.logical_and(origin >= 0, origin < n)
        if moved:
            skipped = jnp.logical_and(jnp.logical_not(own), jnp.logical_and(at_end, r >= kept))
            valid = jnp.logical_and(valid, jnp.logical_not(skipped))
        return origin, r, side, jnp.logical_not(own), valid

    @pl.loop(0, steps)
    def _(u):
        origin, r, side, foreign, valid = place(u)

        if moved:

            @pl.when(jnp.logical_and(near_end, u == kept))
            def _():
                @pl.loop(0, moved)
                def _(g):
                    for copy in peer_copies(g, lane_me, lane_me):
                        copy.wait_recv()

                    @pl.loop(1, peers)
                    def _(k):
                        for copy in peer_copies(g, lane_me, lax.rem(lane_me + k, peers)):
                            copy.start()

            @pl.when(jnp.logical_and(near_end, u == 3 * kept))
            def _():
                @pl.loop(0, moved)
                def _(g):
                    @pl.loop(1, peers)
                    def _(k):
                        j = lax.rem(lane_me + k, peers)
                        for copy in peer_copies(g, j, lane_me):
                            copy.wait_recv()

        @pl.when(jnp.logical_and(foreign, valid))
        def _():
            hop_copy(origin, r, side).wait_recv()

            @pl.when(sends_on(r, side))
            def _():
                hop_copy(origin, r, side).start()

        @pl.when(valid)
        def _():
            q = qbuf[origin, r].T
            top, summed, acc = stats(page_scores(q, r, r, me), lat[r])
            top_ref[...] = top
            sum_ref[...] = summed
            acc_ref[...] = acc
            if moved:
                away = jnp.logical_and(near_end, jnp.logical_and(r >= kept, origin != end_side))

                @pl.when(away)
                def _():
                    extra = r + moved
                    top_x, sum_x, acc_x = stats(page_scores(q, extra, r, end_side), lat[extra])
                    top_a = top_ref[...]
                    both = jnp.maximum(top_a, top_x)
                    f_a, f_x = jnp.exp2(top_a - both), jnp.exp2(top_x - both)
                    top_ref[...] = both
                    sum_ref[...] = sum_ref[...] * f_a + sum_x * f_x
                    acc_ref[...] = acc_ref[...] * f_a + acc_x * f_x

            finish(top_ref[...], sum_ref[...], acc_ref[...], origin, mine.at[origin, r])

            @pl.when(foreign)
            def _():
                part_copy(origin, r, me).start()

    def arrives(r, holder):
        if not moved:
            return None
        last = jnp.logical_or(holder == 0, holder == n - 1)
        return jnp.logical_not(jnp.logical_and(last, r >= kept))

    eye = lax.broadcasted_iota(jnp.int32, (nodes, nodes), 0) == lax.broadcasted_iota(
        jnp.int32, (nodes, nodes), 1
    )

    @pl.loop(0, requests)
    def _(r):
        @pl.loop(1, n)
        def _(k):
            holder = lax.rem(me + k, n)
            if moved:

                @pl.when(arrives(r, holder))
                def _():
                    part_copy(me, r, holder).wait_recv()

            else:
                part_copy(me, r, holder).wait_recv()

        def lse_of(stat):
            stat = stat.astype(jnp.float32)
            lse = stat + pltpu.roll(stat, LANES - heads, 1) + pltpu.roll(stat, LANES - 2 * heads, 1)
            return jnp.where(lane < heads, lse, NEGATIVE)

        own = mine[me, r]
        own_lse = lse_of(own[:, width:])
        top = lax.fori_loop(
            0,
            n,
            lambda k, best: jnp.maximum(best, lse_of(parts[k, r, :, width : width + LANES])),
            own_lse,
            unroll=n <= 8,
        )
        top = jnp.where(lane < heads, top, 0.0)

        def add(carried, lse, part):
            weight_sum, summed = carried
            weight = jnp.exp2(lse - top)
            spread = jnp.concatenate(
                [jnp.broadcast_to(weight[:, h : h + 1], (nodes, dim_v)) for h in range(heads)], axis=1
            )
            return weight_sum + spread, summed + spread * part.astype(jnp.float32)

        zero = jnp.zeros((nodes, width), jnp.float32)
        weight_sum, summed = lax.fori_loop(
            0,
            n,
            lambda k, carried: add(
                carried, lse_of(parts[k, r, :, width : width + LANES]), parts[k, r, :, :width]
            ),
            add((zero, zero), own_lse, own[:, :width]),
            unroll=n <= 8,
        )
        alive = alive_ref[pl.ds(r, 1), :].astype(jnp.float32)
        alive = jnp.sum(jnp.where(eye, alive, 0.0), axis=1, keepdims=True)
        out_ref[r] = (summed / weight_sum * alive).astype(out_ref.dtype)

    if moved:

        @pl.when(at_end)
        def _():
            @pl.loop(0, moved)
            def _(g):
                for copy in page_copies(g):
                    copy.wait_send()

        @pl.when(near_end)
        def _():
            @pl.loop(0, moved)
            def _(g):
                @pl.loop(1, peers)
                def _(k):
                    for copy in peer_copies(g, lane_me, lax.rem(lane_me + k, peers)):
                        copy.wait_send()

    @pl.loop(0, requests)
    def _(r):
        for side in (0, 1):

            @pl.when(sends_on(r, side))
            def _():
                own_copy(r, side).wait_send()

    @pl.loop(0, steps)
    def _(u):
        origin, r, side, foreign, valid = place(u)

        @pl.when(jnp.logical_and(foreign, valid))
        def _():
            @pl.when(sends_on(r, side))
            def _():
                hop_copy(origin, r, side).wait_send()

            part_copy(origin, r, me).wait_send()


def shards(
    queries,
    tree_keys,
    parents,
    node_live,
    lengths,
    start_device,
    cache_latent,
    cache_rope,
    up_weight,
):
    n = lax.axis_size("blk")
    requests, dim_q, cols = queries.shape
    nodes = tree_keys.shape[1]
    _, page, dim_lat = cache_latent.shape
    dim_rope = cache_rope.shape[1]
    dim_v = up_weight.shape[2]
    width = cols // nodes * dim_v
    bf16 = jnp.bfloat16
    scale = math.log2(math.e) / math.sqrt(DN + dim_rope)
    peers = lax.axis_size("head")
    movable = n >= 4 and page % (peers * LANES) == 0
    moved = max(requests // 4, 1) if movable else 0
    slots = max(moved, 1)
    vmem = pl.BlockSpec(memory_space=pltpu.VMEM)
    smem = pl.BlockSpec(memory_space=pltpu.SMEM)
    anywhere = pl.BlockSpec(memory_space=pl.ANY)
    return pl.pallas_call(
        functools.partial(kernel, n, peers, moved, scale),
        out_shape=jax.ShapeDtypeStruct((requests, nodes, width), bf16),
        in_specs=[anywhere, vmem, vmem, vmem, smem, smem, anywhere, anywhere, anywhere],
        out_specs=vmem,
        scratch_shapes=[
            pltpu.VMEM((n, requests, dim_q, cols), bf16),
            pltpu.VMEM((requests + moved, page, dim_lat), bf16),
            pltpu.VMEM((requests + moved, dim_rope, page), bf16),
            pltpu.VMEM(up_weight.shape, bf16),
            pltpu.VMEM((n, requests, nodes, width + LANES), bf16),
            pltpu.VMEM((n, requests, nodes, width + LANES), bf16),
            pltpu.VMEM((requests, nodes, requests * nodes), jnp.float32),
            pltpu.VMEM((cols, 1), jnp.float32),
            pltpu.VMEM((cols, 1), jnp.float32),
            pltpu.VMEM((cols, dim_lat), jnp.float32),
            pltpu.SemaphoreType.DMA((3, requests)),
            pltpu.SemaphoreType.DMA,
            pltpu.SemaphoreType.DMA((2, n, requests)),
            pltpu.SemaphoreType.DMA((n, requests)),
            pltpu.SemaphoreType.DMA((n, requests)),
            pltpu.SemaphoreType.DMA((n, requests)),
            pltpu.SemaphoreType.DMA((2, slots)),
            pltpu.SemaphoreType.DMA((2, slots, peers)),
            pltpu.SemaphoreType.DMA((2, slots, peers)),
        ],
        compiler_params=pltpu.CompilerParams(
            collective_id=0, has_side_effects=True, vmem_limit_bytes=60 * 1024 * 1024
        ),
        name="tree_attention",
    )(
        queries,
        tree_keys,
        parents,
        node_live,
        lengths,
        start_device,
        cache_latent,
        cache_rope,
        up_weight,
    )


def solution(mesh):
    return jax.shard_map(
        shards,
        mesh=mesh,
        in_specs=(
            P("grp", None, ("head", "blk")),
            P("grp", None, None),
            P("grp", None),
            P("grp", None),
            P("grp"),
            P("grp"),
            P("grp", "blk", None),
            P("grp", None, "blk"),
            P("head", None, None),
        ),
        out_specs=P("grp", None, ("head", "blk")),
        check_vma=False,
    )
```

profile of v0, /device:TPU:0, one launch (start us, length us, event | category | flops | bytes accessed | tf_op | source)
XLA Modules:
  0.0 92.1 jit_solution(10578327559375519818)
XLA Ops:
  0.0 90.5 %tree_attention.1 = bf16[4,32,1024]{2,1,0:T(8,128)(2,1)} custom-call(bf16[4,576,256]{2,1,0:T(8,128)(2,1)} %q_hbm.1, bf16[4,32,576]{2,1,0:T(8,128)(2,1)} %tree_ref.1, s32[4,32]{1,0:T(4,128)} %parent_ref.1, s32[4,32]{1,0:T(4,128)} %alive_ref.1, s32[4]{0:T(128)} %length_ref.1, s32[4]{0:T(128)} %first_ref.1, bf16[4,1536,512]{2,1,0:T(8,128)(2,1)} %lat_hbm.1, ...), custom_call_target="tpu_custom_call" | custom-call | tf_op jit(solution)/shard_map/tree_attention/pallas_call | solution.py:491
  90.5 1.7 %copy.11 = bf16[4,32,1024]{2,1,0:T(8,128)(2,1)} copy(bf16[4,32,1024]{2,1,0:T(8,128)(2,1)} %tree_attention.1) | data formatting | bytes 524288
where the time goes:
time: 92.3 us; the launch traced here: 92.1 us
  Pallas kernels  90.5 us (98%)
  local copies, waits for them, and re-layouts  1.67 us (2%)
    pallas_call x1, Pallas kernels, shards(): pl.pallas_call(functools.partial(kernel, n, peers, moved, scale), out_sha...  90.5 us

commit v1 on v0

--- a/solution.py
+++ b/solution.py
@@ -130,21 +130,57 @@
             ),
         )
 
-    def peer_copies(g, j, peer):
-        share_rows = rows_of(j)
-        return tuple(
+    stages = []
+    while moved and (peers >> len(stages)) > 1:
+        stages.append(peers >> (len(stages) + 1))
+
+    def partner(j, gap):
+        return j + gap * (1 - 2 * lax.rem(j // gap, 2))
+
+    def held(stage):
+        slices = [lane_me]
+        for gap in stages[:stage]:
+            slices = slices + [partner(j, gap) for j in slices]
+        return slices
+
+    def share_copies(g, stage):
+        target = partner(lane_me, stages[stage])
+        pieces = held(stage)
+        return [
             pltpu.make_async_remote_copy(
                 src_ref=view,
                 dst_ref=view,
-                send_sem=peer_send.at[i, g, peer],
+                send_sem=peer_send.at[i, g, len(pieces) - 1 + at],
                 recv_sem=page_recv.at[i, g, j],
-                device_id={"head": peer},
+                device_id={"head": target},
                 device_id_type=mesh_id,
             )
+            for at, j in enumerate(pieces)
             for i, view in enumerate(
-                (lat.at[requests + g, share_rows], rope.at[requests + g, :, share_rows])
+                (lat.at[requests + g, rows_of(j)], rope.at[requests + g, :, rows_of(j)])
             )
-        )
+        ]
+
+    def await_pieces(g, pieces):
+        for j in pieces:
+            for i, view in enumerate(
+                (lat.at[requests + g, rows_of(j)], rope.at[requests + g, :, rows_of(j)])
+            ):
+                pltpu.make_async_remote_copy(
+                    src_ref=view,
+                    dst_ref=view,
+                    send_sem=page_send.at[i, g],
+                    recv_sem=page_recv.at[i, g, j],
+                    device_id={"blk": me},
+                    device_id_type=mesh_id,
+                ).wait_recv()
+
+    def share_stage(g, stage):
+        pieces = held(stage)
+        await_pieces(g, pieces[len(pieces) // 2 :])
+        if stage < len(stages):
+            for copy in share_copies(g, stage):
+                copy.start()
 
     barrier = pltpu.get_barrier_semaphore()
 
@@ -277,88 +313,97 @@
         top, summed, acc = stats(s, keys[:, :dim_lat])
         finish(top, summed, acc, me, parts.at[me, r])
 
-    near = 2 * requests
-    steps = near * (n - 1) + requests
-
-    def place(u):
-        v = u - kept
-        late = v >= near
-        own = jnp.logical_or(v < 0, jnp.logical_and(late, v < near + moved))
-        t = jnp.where(late, v - moved, jnp.maximum(v, 0))
-        d = t // near + 1
-        side = lax.rem(t, 2)
-        r = jnp.where(
-            own, jnp.where(late, kept + v - near, u), lax.rem(t // 2, requests)
-        )
+    flipped = jnp.where(2 * me < n, 1, 0)
+
+    def place(u, first, count):
+        t = jnp.maximum(u - count, 0)
+        own = u < count
+        d = t // (2 * count) + 1
+        side = lax.rem(t // count + flipped, 2)
+        r = first + lax.rem(u, count)
         origin = jnp.where(own, me, me - d + 2 * d * side)
         valid = jnp.logical_and(origin >= 0, origin < n)
-        if moved:
-            skipped = jnp.logical_and(jnp.logical_not(own), jnp.logical_and(at_end, r >= kept))
-            valid = jnp.logical_and(valid, jnp.logical_not(skipped))
+        if first:
+            valid = jnp.logical_and(valid, jnp.logical_or(own, jnp.logical_not(at_end)))
         return origin, r, side, jnp.logical_not(own), valid
 
-    @pl.loop(0, steps)
-    def _(u):
-        origin, r, side, foreign, valid = place(u)
-
-        if moved:
-
-            @pl.when(jnp.logical_and(near_end, u == kept))
-            def _():
-                @pl.loop(0, moved)
-                def _(g):
-                    for copy in peer_copies(g, lane_me, lane_me):
-                        copy.wait_recv()
-
-                    @pl.loop(1, peers)
-                    def _(k):
-                        for copy in peer_copies(g, lane_me, lax.rem(lane_me + k, peers)):
-                            copy.start()
-
-            @pl.when(jnp.logical_and(near_end, u == 3 * kept))
-            def _():
-                @pl.loop(0, moved)
-                def _(g):
-                    @pl.loop(1, peers)
-                    def _(k):
-                        j = lax.rem(lane_me + k, peers)
-                        for copy in peer_copies(g, j, lane_me):
-                            copy.wait_recv()
-
-        @pl.when(jnp.logical_and(foreign, valid))
+    classes = [(0, kept)] + ([(kept, moved)] if moved else [])
+
+    def events(first, u):
+        if not moved:
+            return
+        if first:
+
+            @pl.when(jnp.logical_and(near_end, u == 0))
+            def _():
+                for stage in range(2, len(stages) + 1):
+                    for g in range(moved):
+                        share_stage(g, stage)
+                if len(stages) == 1:
+                    for g in range(moved):
+                        share_stage(g, 1)
+
+            return
+
+        @pl.when(jnp.logical_and(near_end, u == kept + 1))
         def _():
-            hop_copy(origin, r, side).wait_recv()
-
-            @pl.when(sends_on(r, side))
-            def _():
-                hop_copy(origin, r, side).start()
-
-        @pl.when(valid)
+            share_stage(0, 0)
+
+        @pl.when(jnp.logical_and(near_end, u == 2 * kept))
         def _():
-            q = qbuf[origin, r].T
-            top, summed, acc = stats(page_scores(q, r, r, me), lat[r])
-            top_ref[...] = top
-            sum_ref[...] = summed
-            acc_ref[...] = acc
-            if moved:
-                away = jnp.logical_and(near_end, jnp.logical_and(r >= kept, origin != end_side))
-
-                @pl.when(away)
+            for g in range(1, moved):
+                share_stage(g, 0)
+            if len(stages) > 1:
+                share_stage(0, 1)
+
+        @pl.when(jnp.logical_and(near_end, u == 3 * kept))
+        def _():
+            if len(stages) > 1:
+                for g in range(1, moved):
+                    share_stage(g, 1)
+
+    for first, count in classes:
+
+        @pl.loop(0, count * (2 * n - 1))
+        def _(u):
+            origin, r, side, foreign, valid = place(u, first, count)
+            events(first, u)
+
+            @pl.when(jnp.logical_and(foreign, valid))
+            def _():
+                hop_copy(origin, r, side).wait_recv()
+
+                @pl.when(sends_on(r, side))
                 def _():
-                    extra = r + moved
-                    top_x, sum_x, acc_x = stats(page_scores(q, extra, r, end_side), lat[extra])
-                    top_a = top_ref[...]
-                    both = jnp.maximum(top_a, top_x)
-                    f_a, f_x = jnp.exp2(top_a - both), jnp.exp2(top_x - both)
-                    top_ref[...] = both
-                    sum_ref[...] = sum_ref[...] * f_a + sum_x * f_x
-                    acc_ref[...] = acc_ref[...] * f_a + acc_x * f_x
-
-            finish(top_ref[...], sum_ref[...], acc_ref[...], origin, mine.at[origin, r])
-
-            @pl.when(foreign)
-            def _():
-                part_copy(origin, r, me).start()
+                    hop_copy(origin, r, side).start()
+
+            @pl.when(valid)
+            def _():
+                q = qbuf[origin, r].T
+                top, summed, acc = stats(page_scores(q, r, r, me), lat[r])
+                if first:
+                    top_ref[...] = top
+                    sum_ref[...] = summed
+                    acc_ref[...] = acc
+
+                    @pl.when(jnp.logical_and(near_end, origin != end_side))
+                    def _():
+                        extra = r + moved
+                        top_x, sum_x, acc_x = stats(page_scores(q, extra, r, end_side), lat[extra])
+                        top_a = top_ref[...]
+                        both = jnp.maximum(top_a, top_x)
+                        f_a, f_x = jnp.exp2(top_a - both), jnp.exp2(top_x - both)
+                        top_ref[...] = both
+                        sum_ref[...] = sum_ref[...] * f_a + sum_x * f_x
+                        acc_ref[...] = acc_ref[...] * f_a + acc_x * f_x
+
+                    top, summed, acc = top_ref[...], sum_ref[...], acc_ref[...]
+
+                finish(top, summed, acc, origin, mine.at[origin, r])
+
+                @pl.when(foreign)
+                def _():
+                    part_copy(origin, r, me).start()
 
     def arrives(r, holder):
         if not moved:
@@ -435,9 +480,8 @@
         def _():
             @pl.loop(0, moved)
             def _(g):
-                @pl.loop(1, peers)
-                def _(k):
-                    for copy in peer_copies(g, lane_me, lax.rem(lane_me + k, peers)):
+                for stage in range(len(stages)):
+                    for copy in share_copies(g, stage):
                         copy.wait_send()
 
     @pl.loop(0, requests)
@@ -448,17 +492,19 @@
             def _():
                 own_copy(r, side).wait_send()
 
-    @pl.loop(0, steps)
-    def _(u):
-        origin, r, side, foreign, valid = place(u)
-
-        @pl.when(jnp.logical_and(foreign, valid))
-        def _():
-            @pl.when(sends_on(r, side))
-            def _():
-                hop_copy(origin, r, side).wait_send()
-
-            part_copy(origin, r, me).wait_send()
+    for first, count in classes:
+
+        @pl.loop(0, count * (2 * n - 1))
+        def _(u):
+            origin, r, side, foreign, valid = place(u, first, count)
+
+            @pl.when(jnp.logical_and(foreign, valid))
+            def _():
+                @pl.when(sends_on(r, side))
+                def _():
+                    hop_copy(origin, r, side).wait_send()
+
+                part_copy(origin, r, me).wait_send()
 
 
 def shards(
@@ -482,8 +528,8 @@
     bf16 = jnp.bfloat16
     scale = math.log2(math.e) / math.sqrt(DN + dim_rope)
     peers = lax.axis_size("head")
-    movable = n >= 4 and page % (peers * LANES) == 0
-    moved = max(requests // 4, 1) if movable else 0
+    movable = n >= 4 and peers & (peers - 1) == 0 < peers - 1 and page % (peers * LANES) == 0
+    moved = requests // 2 if movable else 0
     slots = max(moved, 1)
     vmem = pl.BlockSpec(memory_space=pltpu.VMEM)
     smem = pl.BlockSpec(memory_space=pltpu.SMEM)

time: 92.3 us -> 93.5 us (1.013)
  Pallas kernels: 90.5 us -> 91.6 us
    pallas_call x1, Pallas kernels: 90.5 us -> 91.6 us  [shards(): pl.pallas_call(functools.partial(kernel, n, peers, moved, scale), out_sha...]
where the time goes in v1:
time: 93.5 us; the launch traced here: 93.3 us
  Pallas kernels  91.6 us (98%)
  local copies, waits for them, and re-layouts  1.67 us (2%)
    pallas_call x1, Pallas kernels, shards(): pl.pallas_call(functools.partial(kernel, n, peers, moved, scale), out_sha...  91.6 us

profile of v1, /device:TPU:0, one launch (start us, length us, event | category | flops | bytes accessed | tf_op | source)
XLA Modules:
  0.0 93.3 jit_solution(10226523740903609255)
XLA Ops:
  0.0 91.6 %tree_attention.1 = bf16[4,32,1024]{2,1,0:T(8,128)(2,1)} custom-call(bf16[4,576,256]{2,1,0:T(8,128)(2,1)} %q_hbm.1, bf16[4,32,576]{2,1,0:T(8,128)(2,1)} %tree_ref.1, s32[4,32]{1,0:T(4,128)} %parent_ref.1, s32[4,32]{1,0:T(4,128)} %alive_ref.1, s32[4]{0:T(128)} %length_ref.1, s32[4]{0:T(128)} %first_ref.1, bf16[4,1536,512]{2,1,0:T(8,128)(2,1)} %lat_hbm.1, ...), custom_call_target="tpu_custom_call" | custom-call | tf_op jit(solution)/shard_map/tree_attention/pallas_call | solution.py:537
  91.7 1.7 %copy.11 = bf16[4,32,1024]{2,1,0:T(8,128)(2,1)} copy(bf16[4,32,1024]{2,1,0:T(8,128)(2,1)} %tree_attention.1) | data formatting | bytes 524288

commit v2 on v1

--- a/solution.py
+++ b/solution.py
@@ -30,8 +30,9 @@
     w_hbm,
     out_ref,
     qbuf,
-    lat,
+    keyed,
     rope,
+    valued,
     w,
     parts,
     mine,
@@ -51,10 +52,10 @@
 ):
     me = lax.axis_index("blk")
     lane_me = lax.axis_index("head")
-    requests, _, cols = q_hbm.shape
+    requests, dim_q, cols = q_hbm.shape
     nodes = tree_ref.shape[1]
-    dim_lat = lat.shape[2]
-    page = lat.shape[1]
+    page, dim_lat = lat_hbm.shape[1:]
+    dim_pad = keyed.shape[2]
     dim_v = w.shape[2]
     heads = cols // nodes
     width = heads * dim_v
@@ -65,10 +66,13 @@
     near_end = jnp.logical_or(me == 1, me == n - 2)
     end_side = jnp.where(me <= 1, 0, n - 1)
 
+    def chunk(origin, r):
+        return qbuf.at[origin, r, :dim_q]
+
     def load_copies(r):
         return (
-            pltpu.make_async_copy(q_hbm.at[r], qbuf.at[me, r], load_sem.at[0, r]),
-            pltpu.make_async_copy(lat_hbm.at[r], lat.at[r], load_sem.at[1, r]),
+            pltpu.make_async_copy(q_hbm.at[r], chunk(me, r), load_sem.at[0, r]),
+            pltpu.make_async_copy(lat_hbm.at[r], keyed.at[r, :, :dim_lat], load_sem.at[1, r]),
             pltpu.make_async_copy(rope_hbm.at[r], rope.at[r], load_sem.at[2, r]),
         )
 
@@ -78,7 +82,7 @@
     def own_copy(r, side):
         return pltpu.make_async_remote_copy(
             src_ref=q_hbm.at[r],
-            dst_ref=qbuf.at[me, r],
+            dst_ref=chunk(me, r),
             send_sem=q_send.at[side, me, r],
             recv_sem=q_recv.at[me, r],
             device_id={"blk": me + 1 - 2 * side},
@@ -87,8 +91,8 @@
 
     def hop_copy(origin, r, side):
         return pltpu.make_async_remote_copy(
-            src_ref=qbuf.at[origin, r],
-            dst_ref=qbuf.at[origin, r],
+            src_ref=chunk(origin, r),
+            dst_ref=chunk(origin, r),
             send_sem=q_send.at[side, origin, r],
             recv_sem=q_recv.at[origin, r],
             device_id={"blk": me + 1 - 2 * side},
@@ -114,7 +118,7 @@
         return (
             pltpu.make_async_remote_copy(
                 src_ref=lat_hbm.at[kept + g, mine_rows],
-                dst_ref=lat.at[requests + g, mine_rows],
+                dst_ref=keyed.at[requests + g, mine_rows, :dim_lat],
                 send_sem=page_send.at[0, g],
                 recv_sem=page_recv.at[0, g, lane_me],
                 device_id={"blk": inner},
@@ -157,14 +161,14 @@
             )
             for at, j in enumerate(pieces)
             for i, view in enumerate(
-                (lat.at[requests + g, rows_of(j)], rope.at[requests + g, :, rows_of(j)])
+                (keyed.at[requests + g, rows_of(j), :dim_lat], rope.at[requests + g, :, rows_of(j)])
             )
         ]
 
     def await_pieces(g, pieces):
         for j in pieces:
             for i, view in enumerate(
-                (lat.at[requests + g, rows_of(j)], rope.at[requests + g, :, rows_of(j)])
+                (keyed.at[requests + g, rows_of(j), :dim_lat], rope.at[requests + g, :, rows_of(j)])
             ):
                 pltpu.make_async_remote_copy(
                     src_ref=view,
@@ -245,7 +249,14 @@
     for _ in range(max(nodes - 1, 1).bit_length()):
         factor = reached.astype(jnp.bfloat16)
         reached = jnp.minimum(jnp.dot(factor, factor, preferred_element_type=jnp.float32), 1.0)
-    reach[...] = reached.T.reshape(requests, nodes, total)
+    reach[...] = reached.astype(jnp.bfloat16)
+
+    @pl.loop(0, n)
+    def _(origin):
+        @pl.loop(0, requests)
+        def _(r):
+            pad = lax.broadcasted_iota(jnp.int32, (dim_pad - dim_q, cols), 0)
+            qbuf[origin, r, dim_q:] = jnp.where(pad == 0, 1.0, 0.0).astype(jnp.bfloat16)
 
     if moved:
         for end in (0, n - 1):
@@ -258,28 +269,34 @@
                     blank[:, :width] = jnp.zeros((nodes, width), jnp.bfloat16)
                     blank[:, width:] = jnp.where(lane < heads, NEGATIVE, 0.0).astype(jnp.bfloat16)
 
-    def stats(scores, values):
-        top = jnp.maximum(jnp.max(scores, axis=1, keepdims=True), FLOOR)
-        weights = jnp.exp2(scores - top)
-        summed = jnp.sum(weights, axis=1, keepdims=True)
-        acc = jnp.dot(weights.astype(jnp.bfloat16), values, preferred_element_type=jnp.float32)
-        return top, summed, acc
-
-    def page_scores(q, place, r, holder):
-        s = lax.dot_general(
-            q[:, :dim_lat], lat[place], (((1,), (1,)), ((), ())), preferred_element_type=jnp.float32
-        )
-        s = s + jnp.dot(q[:, dim_lat:], rope[place], preferred_element_type=jnp.float32)
+    def prepare(place, r, holder):
         turn = lax.rem(holder - first_ref[r] + n, n)
         live = length_ref[r] - turn * page
-        slot = lax.broadcasted_iota(jnp.int32, (1, page), 1)
-        return jnp.where(slot < live, s * scale, NEGATIVE)
+        shape = (page, dim_pad - dim_q)
+        slot = lax.broadcasted_iota(jnp.int32, shape, 0)
+        pad = lax.broadcasted_iota(jnp.int32, shape, 1)
+        hide = jnp.where(jnp.logical_and(pad == 0, slot >= live), NEGATIVE, 0.0)
+        keyed[place, :, dim_lat:] = jnp.concatenate(
+            [rope[place].T, hide.astype(jnp.bfloat16)], axis=1
+        )
+        valued[place] = keyed[place, :, :dim_lat].T
+
+    def stats(scores, values):
+        top = jnp.maximum(jnp.max(scores, axis=0, keepdims=True), FLOOR)
+        weights = jnp.exp2((scores - top) * scale)
+        summed = jnp.sum(weights, axis=0, keepdims=True)
+        acc = jnp.dot(values, weights.astype(jnp.bfloat16), preferred_element_type=jnp.float32)
+        return top, summed, acc
+
+    def page_stats(place, q):
+        return stats(jnp.dot(keyed[place], q, preferred_element_type=jnp.float32), valued[place])
 
     def finish(top, summed, acc, origin, dst):
         any_kept = summed > 0.0
         safe = jnp.where(any_kept, summed, 1.0)
-        rows = (acc * jnp.where(any_kept, 1.0 / safe, 0.0)).astype(jnp.bfloat16)
-        lse = jnp.where(any_kept, top + jnp.log2(safe), NEGATIVE)
+        rows = (acc * jnp.where(any_kept, 1.0 / safe, 0.0)).astype(jnp.bfloat16).T
+        lse = jnp.where(any_kept, top * scale + jnp.log2(safe), NEGATIVE)
+        lse = jnp.broadcast_to(lse, (LANES, cols)).T
         stat = jnp.zeros((nodes, LANES), jnp.float32)
         for h in range(heads):
             span = slice(h * nodes, (h + 1) * nodes)
@@ -305,12 +322,15 @@
     def _(r):
         for copy in load_copies(r):
             copy.wait()
-        q = qbuf[me, r].T
-        keys = tree_ref[...].reshape(total, tree_ref.shape[2])
-        s = lax.dot_general(q, keys, (((1,), (1,)), ((), ())), preferred_element_type=jnp.float32)
-        seen = jnp.concatenate([reach[r]] * heads, axis=0) > 0.5
-        s = jnp.where(seen, s * scale, NEGATIVE)
-        top, summed, acc = stats(s, keys[:, :dim_lat])
+        prepare(r, r, me)
+        q = qbuf[me, r, :dim_q]
+        keys = tree_ref[...].reshape(total, dim_q)
+        s = jnp.dot(keys, q, preferred_element_type=jnp.float32)
+        node = r * nodes + lax.rem(lax.broadcasted_iota(jnp.int32, (total, cols), 1), nodes)
+        spread = jnp.where(lax.broadcasted_iota(jnp.int32, (total, cols), 0) == node, 1.0, 0.0)
+        seen = jnp.dot(reach[...], spread.astype(jnp.bfloat16), preferred_element_type=jnp.float32)
+        s = jnp.where(seen > 0.5, s, NEGATIVE)
+        top, summed, acc = stats(s, keys[:, :dim_lat].T)
         finish(top, summed, acc, me, parts.at[me, r])
 
     flipped = jnp.where(2 * me < n, 1, 0)
@@ -343,6 +363,10 @@
                     for g in range(moved):
                         share_stage(g, 1)
 
+                @pl.loop(0, moved)
+                def _(g):
+                    prepare(requests + g, kept + g, end_side)
+
             return
 
         @pl.when(jnp.logical_and(near_end, u == kept + 1))
@@ -379,8 +403,7 @@
 
             @pl.when(valid)
             def _():
-                q = qbuf[origin, r].T
-                top, summed, acc = stats(page_scores(q, r, r, me), lat[r])
+                top, summed, acc = page_stats(r, qbuf[origin, r])
                 if first:
                     top_ref[...] = top
                     sum_ref[...] = summed
@@ -388,11 +411,11 @@
 
                     @pl.when(jnp.logical_and(near_end, origin != end_side))
                     def _():
-                        extra = r + moved
-                        top_x, sum_x, acc_x = stats(page_scores(q, extra, r, end_side), lat[extra])
+                        top_x, sum_x, acc_x = page_stats(r + moved, qbuf[origin, r])
                         top_a = top_ref[...]
                         both = jnp.maximum(top_a, top_x)
-                        f_a, f_x = jnp.exp2(top_a - both), jnp.exp2(top_x - both)
+                        f_a = jnp.exp2((top_a - both) * scale)
+                        f_x = jnp.exp2((top_x - both) * scale)
                         top_ref[...] = both
                         sum_ref[...] = sum_ref[...] * f_a + sum_x * f_x
                         acc_ref[...] = acc_ref[...] * f_a + acc_x * f_x
@@ -527,6 +550,7 @@
     width = cols // nodes * dim_v
     bf16 = jnp.bfloat16
     scale = math.log2(math.e) / math.sqrt(DN + dim_rope)
+    dim_pad = (dim_q // LANES + 1) * LANES
     peers = lax.axis_size("head")
     movable = n >= 4 and peers & (peers - 1) == 0 < peers - 1 and page % (peers * LANES) == 0
     moved = requests // 2 if movable else 0
@@ -540,16 +564,17 @@
         in_specs=[anywhere, vmem, vmem, vmem, smem, smem, anywhere, anywhere, anywhere],
         out_specs=vmem,
         scratch_shapes=[
-            pltpu.VMEM((n, requests, dim_q, cols), bf16),
-            pltpu.VMEM((requests + moved, page, dim_lat), bf16),
+            pltpu.VMEM((n, requests, dim_pad, cols), bf16),
+            pltpu.VMEM((requests + moved, page, dim_pad), bf16),
             pltpu.VMEM((requests + moved, dim_rope, page), bf16),
+            pltpu.VMEM((requests + moved, dim_lat, page), bf16),
             pltpu.VMEM(up_weight.shape, bf16),
             pltpu.VMEM((n, requests, nodes, width + LANES), bf16),
             pltpu.VMEM((n, requests, nodes, width + LANES), bf16),
-            pltpu.VMEM((requests, nodes, requests * nodes), jnp.float32),
-            pltpu.VMEM((cols, 1), jnp.float32),
-            pltpu.VMEM((cols, 1), jnp.float32),
-            pltpu.VMEM((cols, dim_lat), jnp.float32),
+            pltpu.VMEM((requests * nodes, requests * nodes), bf16),
+            pltpu.VMEM((1, cols), jnp.float32),
+            pltpu.VMEM((1, cols), jnp.float32),
+            pltpu.VMEM((dim_lat, cols), jnp.float32),
             pltpu.SemaphoreType.DMA((3, requests)),
             pltpu.SemaphoreType.DMA,
             pltpu.SemaphoreType.DMA((2, n, requests)),

time: 93.5 us -> 103 us (1.10)
  Pallas kernels: 91.6 us -> 101 us
    pallas_call x1, Pallas kernels: 91.6 us -> 101 us  [shards(): pl.pallas_call(functools.partial(kernel, n, peers, moved, scale), out_sha...]
where the time goes in v2:
time: 103 us
  Pallas kernels  101 us (98%)
  local copies, waits for them, and re-layouts  1.67 us (2%)
    pallas_call x1, Pallas kernels, shards(): pl.pallas_call(functools.partial(kernel, n, peers, moved, scale), out_sha...  101 us

profile of v2, /device:TPU:0, one launch (start us, length us, event | category | flops | bytes accessed | tf_op | source)
XLA Modules:
  0.0 103.0 jit_solution(17008114117605609710)
XLA Ops:
  0.0 101.3 %tree_attention.1 = bf16[4,32,1024]{2,1,0:T(8,128)(2,1)} custom-call(bf16[4,576,256]{2,1,0:T(8,128)(2,1)} %q_hbm.1, bf16[4,32,576]{2,1,0:T(8,128)(2,1)} %tree_ref.1, s32[4,32]{1,0:T(4,128)} %parent_ref.1, s32[4,32]{1,0:T(4,128)} %alive_ref.1, s32[4]{0:T(128)} %length_ref.1, s32[4]{0:T(128)} %first_ref.1, bf16[4,1536,512]{2,1,0:T(8,128)(2,1)} %lat_hbm.1, ...), custom_call_target="tpu_custom_call" | custom-call | tf_op jit(solution)/shard_map/tree_attention/pallas_call | solution.py:561
  101.3 1.7 %copy.11 = bf16[4,32,1024]{2,1,0:T(8,128)(2,1)} copy(bf16[4,32,1024]{2,1,0:T(8,128)(2,1)} %tree_attention.1) | data formatting | bytes 524288

commit v3 on v1

--- a/solution.py
+++ b/solution.py
@@ -226,13 +226,18 @@
                 for copy in page_copies(g):
                     copy.start()
 
-    @pl.loop(0, requests)
-    def _(r):
-        for side in (0, 1):
-
-            @pl.when(sends_on(r, side))
-            def _():
-                own_copy(r, side).start()
+    def send_own():
+        @pl.loop(0, requests)
+        def _(r):
+            for side in (0, 1):
+
+                @pl.when(sends_on(r, side))
+                def _():
+                    own_copy(r, side).start()
+
+    @pl.when(jnp.logical_not(at_end) if moved else me >= 0)
+    def _():
+        send_own()
 
     lane = lax.broadcasted_iota(jnp.int32, (nodes, LANES), 1)
     total = requests * nodes
@@ -345,6 +350,15 @@
 
             return
 
+        @pl.when(jnp.logical_and(at_end, u == kept))
+        def _():
+            @pl.loop(0, moved)
+            def _(g):
+                for copy in page_copies(g):
+                    copy.wait_send()
+
+            send_own()
+
         @pl.when(jnp.logical_and(near_end, u == kept + 1))
         def _():
             share_stage(0, 0)
@@ -468,13 +482,6 @@
         out_ref[r] = (summed / weight_sum * alive).astype(out_ref.dtype)
 
     if moved:
-
-        @pl.when(at_end)
-        def _():
-            @pl.loop(0, moved)
-            def _(g):
-                for copy in page_copies(g):
-                    copy.wait_send()
 
         @pl.when(near_end)
         def _():

time: 93.5 us -> 92.8 us (level)
  no operation moved by 1% of the time
where the time goes in v3:
time: 92.8 us; the launch traced here: 92.7 us
  Pallas kernels  91 us (98%)
  local copies, waits for them, and re-layouts  1.67 us (2%)
    pallas_call x1, Pallas kernels, shards(): pl.pallas_call(functools.partial(kernel, n, peers, moved, scale), out_sha...  91 us

profile of v3, /device:TPU:0, one launch (start us, length us, event | category | flops | bytes accessed | tf_op | source)
XLA Modules:
  0.0 92.7 jit_solution(9613522570600922330)
XLA Ops:
  0.0 91.0 %tree_attention.1 = bf16[4,32,1024]{2,1,0:T(8,128)(2,1)} custom-call(bf16[4,576,256]{2,1,0:T(8,128)(2,1)} %q_hbm.1, bf16[4,32,576]{2,1,0:T(8,128)(2,1)} %tree_ref.1, s32[4,32]{1,0:T(4,128)} %parent_ref.1, s32[4,32]{1,0:T(4,128)} %alive_ref.1, s32[4]{0:T(128)} %length_ref.1, s32[4]{0:T(128)} %first_ref.1, bf16[4,1536,512]{2,1,0:T(8,128)(2,1)} %lat_hbm.1, ...), custom_call_target="tpu_custom_call" | custom-call | tf_op jit(solution)/shard_map/tree_attention/pallas_call | solution.py:544
  91.0 1.7 %copy.11 = bf16[4,32,1024]{2,1,0:T(8,128)(2,1)} copy(bf16[4,32,1024]{2,1,0:T(8,128)(2,1)} %tree_attention.1) | data formatting | bytes 524288

commit v4 on v3

--- a/solution.py
+++ b/solution.py
@@ -536,7 +536,7 @@
     scale = math.log2(math.e) / math.sqrt(DN + dim_rope)
     peers = lax.axis_size("head")
     movable = n >= 4 and peers & (peers - 1) == 0 < peers - 1 and page % (peers * LANES) == 0
-    moved = requests // 2 if movable else 0
+    moved = max(requests // 4, 1) if movable else 0
     slots = max(moved, 1)
     vmem = pl.BlockSpec(memory_space=pltpu.VMEM)
     smem = pl.BlockSpec(memory_space=pltpu.SMEM)

time: 92.8 us -> 94.1 us (1.014)
  Pallas kernels: 91 us -> 92.3 us
    pallas_call x1, Pallas kernels: 91 us -> 92.3 us  [shards(): pl.pallas_call(functools.partial(kernel, n, peers, moved, scale), out_sha...]
where the time goes in v4:
time: 94.1 us; the launch traced here: 94 us
  Pallas kernels  92.3 us (98%)
  local copies, waits for them, and re-layouts  1.67 us (2%)
    pallas_call x1, Pallas kernels, shards(): pl.pallas_call(functools.partial(kernel, n, peers, moved, scale), out_sha...  92.3 us

profile of v4, /device:TPU:0, one launch (start us, length us, event | category | flops | bytes accessed | tf_op | source)
XLA Modules:
  0.0 94.0 jit_solution(2840336530632078452)
XLA Ops:
  0.0 92.3 %tree_attention.1 = bf16[4,32,1024]{2,1,0:T(8,128)(2,1)} custom-call(bf16[4,576,256]{2,1,0:T(8,128)(2,1)} %q_hbm.1, bf16[4,32,576]{2,1,0:T(8,128)(2,1)} %tree_ref.1, s32[4,32]{1,0:T(4,128)} %parent_ref.1, s32[4,32]{1,0:T(4,128)} %alive_ref.1, s32[4]{0:T(128)} %length_ref.1, s32[4]{0:T(128)} %first_ref.1, bf16[4,1536,512]{2,1,0:T(8,128)(2,1)} %lat_hbm.1, ...), custom_call_target="tpu_custom_call" | custom-call | tf_op jit(solution)/shard_map/tree_attention/pallas_call | solution.py:544
  92.3 1.7 %copy.11 = bf16[4,32,1024]{2,1,0:T(8,128)(2,1)} copy(bf16[4,32,1024]{2,1,0:T(8,128)(2,1)} %tree_attention.1) | data formatting | bytes 524288

commit v5 on v3

--- a/solution.py
+++ b/solution.py
@@ -376,6 +376,13 @@
                 for g in range(1, moved):
                     share_stage(g, 1)
 
+    def pass_on(origin, r, side):
+        hop_copy(origin, r, side).wait_recv()
+
+        @pl.when(sends_on(r, side))
+        def _():
+            hop_copy(origin, r, side).start()
+
     for first, count in classes:
 
         @pl.loop(0, count * (2 * n - 1))
@@ -383,13 +390,23 @@
             origin, r, side, foreign, valid = place(u, first, count)
             events(first, u)
 
-            @pl.when(jnp.logical_and(foreign, valid))
+            if moved and not first:
+
+                @pl.when(u == 4 * kept)
+                def _():
+                    @pl.loop(moved, 3 * moved)
+                    def _(later):
+                        origin_l, r_l, side_l, _, valid_l = place(later, kept, moved)
+
+                        @pl.when(valid_l)
+                        def _():
+                            pass_on(origin_l, r_l, side_l)
+
+            fresh = jnp.logical_and(foreign, u >= 3 * count) if first else foreign
+
+            @pl.when(jnp.logical_and(fresh, valid))
             def _():
-                hop_copy(origin, r, side).wait_recv()
-
-                @pl.when(sends_on(r, side))
-                def _():
-                    hop_copy(origin, r, side).start()
+                pass_on(origin, r, side)
 
             @pl.when(valid)
             def _():

time: 92.8 us -> 86.1 us (0.928)
  Pallas kernels: 91 us -> 84.2 us
    pallas_call x1, Pallas kernels: 91 us -> 84.2 us  [shards(): pl.pallas_call(functools.partial(kernel, n, peers, moved, scale), out_sha...]
where the time goes in v5:
time: 86.1 us; the launch traced here: 85.9 us
  Pallas kernels  84.2 us (98%)
  local copies, waits for them, and re-layouts  1.67 us (2%)
    pallas_call x1, Pallas kernels, shards(): pl.pallas_call(functools.partial(kernel, n, peers, moved, scale), out_sha...  84.2 us

profile of v5, /device:TPU:0, one launch (start us, length us, event | category | flops | bytes accessed | tf_op | source)
XLA Modules:
  0.0 85.9 jit_solution(16793128877860839491)
XLA Ops:
  0.0 84.2 %tree_attention.1 = bf16[4,32,1024]{2,1,0:T(8,128)(2,1)} custom-call(bf16[4,576,256]{2,1,0:T(8,128)(2,1)} %q_hbm.1, bf16[4,32,576]{2,1,0:T(8,128)(2,1)} %tree_ref.1, s32[4,32]{1,0:T(4,128)} %parent_ref.1, s32[4,32]{1,0:T(4,128)} %alive_ref.1, s32[4]{0:T(128)} %length_ref.1, s32[4]{0:T(128)} %first_ref.1, bf16[4,1536,512]{2,1,0:T(8,128)(2,1)} %lat_hbm.1, ...), custom_call_target="tpu_custom_call" | custom-call | tf_op jit(solution)/shard_map/tree_attention/pallas_call | solution.py:561
  84.2 1.7 %copy.11 = bf16[4,32,1024]{2,1,0:T(8,128)(2,1)} copy(bf16[4,32,1024]{2,1,0:T(8,128)(2,1)} %tree_attention.1) | data formatting | bytes 524288
